TPU v7x, 256 devices: a whole 4x4x8 slice. The times are simulated.
256 devices in a mesh: hist: 32 (over x_hi, z, core), user: 8 (over x_lo, y).
Axes of the slice: x: 4 (x_hi: 2, x_lo: 2; x = x_hi * 2 + x_lo), y: 4, z: 8, core: 2. Of those that a mesh axis runs over, the one named last changes fastest.
Arguments:
- candidate_proj: bfloat16 [8, 2048, 4096], P('user', 'hist'), may hold values from -6 to 6
- history_cache: bfloat16 [32, 128, 512, 256], P('hist', 'user'), may hold values from -6 to 6
- request_owner: int32 [8, 512, 1], P('user', 'hist'), may hold values from 0 to 7; in each aligned block of 16 rows (0 to 15, 16 to 31, ..., all dimensions but the last counted through in order) at most 3 rows name the same one
- request_page: int32 [8, 512], P('user', 'hist'), may hold values from 0 to 15
- history_length: int32 [8], P('user'), may hold values from 1 to 32768, 131080 in all
- candidate_count: int32 [8], P('user'), may hold values from 1 to 2048, 12296 in all
- block_mask: int32 [8, 32, 64], P('user'), may hold values 0 or 1
- norm_gain: float32 [1024], replicated, may hold values from 0.25 to 1.75
- w_out: bfloat16 [1024, 1024], replicated, may hold values from -0.1875 to 0.1875
Outputs:
- candidate_out: bfloat16 [8, 2048, 1024], P('user', 'hist')
Inputs may be any that keep to these rules, and one draw needn't show every extreme that they name: `request_owner`: among the 16 rows of one device, at most 3 name the same owner. `history_length`: the longest history has 32768 events. `candidate_count`: the largest count is 2048.
All inputs are finite; a program needn't handle non-finite values. No bound on the sum of `history_length` or of `candidate_count` or of `block_mask` on one device may be relied on, other than what follows from the above.
Results may differ from a plain program's by a relative error of at most 0.022.
Values may be sent and summed in bfloat16 or wider, within the bound.
A program may use at most 128 MiB of HBM per device.

v0:
```python
import jax
import jax.numpy as jnp
from jax import lax
from jax.sharding import PartitionSpec as P

D = 1024
H = 8
DH = 128
BLK = 512
HB_DEV = 2
CAND_DEV = 64


def fetch_pages(history_cache, request_owner, request_page, needed, capacity, user_count):
    owners = request_owner[0, :, 0]
    page_list = request_page[0]
    slot_index = jnp.arange(needed, dtype=jnp.int32)
    earlier = (owners[:, None] == owners[None, :]) & (slot_index[None, :] < slot_index[:, None])
    ranking = jnp.sum(earlier.astype(jnp.int32), axis=1)
    location = owners * capacity + ranking
    buckets = jnp.arange(user_count * capacity, dtype=jnp.int32)
    matched = location[:, None] == buckets[None, :]
    wanted = (jnp.sum(jnp.where(matched, page_list[:, None] + 1, 0), axis=0) - 1).reshape(
        user_count, capacity
    )
    stored_pages = history_cache[0]
    located = stored_pages[
        jnp.maximum(lax.all_to_all(wanted, "user", split_axis=0, concat_axis=0, tiled=True), 0)
    ]
    fetched = lax.all_to_all(located, "user", split_axis=0, concat_axis=0, tiled=True)
    flattened = fetched.reshape(user_count * capacity, BLK, 2 * DH)
    ordering = jnp.arange(needed, dtype=jnp.int32)
    source_slot = ordering % HB_DEV * H + ordering // HB_DEV
    return flattened[location[source_slot]].reshape(H, HB_DEV * BLK, 2 * DH)


def body(
    candidate_proj,
    history_cache,
    request_owner,
    request_page,
    history_length,
    candidate_count,
    block_mask,
    norm_gain,
    w_out,
):
    hist_count = lax.axis_size("hist")
    user_count = lax.axis_size("user")
    position = lax.axis_index("hist")
    needed = HB_DEV * H
    capacity = max(2, 3 * needed // (2 * user_count))
    events_dev = HB_DEV * BLK
    score_scale = DH ** (-0.5)
    resident = fetch_pages(history_cache, request_owner, request_page, needed, capacity, user_count)
    activated = jax.nn.silu(candidate_proj[0].astype(jnp.float32))
    gating = activated[:, :D]
    cand_values = activated[:, D : 2 * D].astype(jnp.bfloat16)
    queries = activated[:, 2 * D : 3 * D].astype(jnp.bfloat16)
    cand_keys = activated[:, 3 * D :].astype(jnp.bfloat16)
    in_history = (
        position * events_dev + jnp.arange(events_dev, dtype=jnp.int32) < history_length[0]
    ).astype(jnp.float32)
    my_mask = lax.dynamic_slice_in_dim(block_mask[0], position * HB_DEV, HB_DEV, 1).astype(
        jnp.float32
    )
    piece = lax.all_gather(queries, "hist", axis=0, tiled=True)
    row_count = piece.shape[0]
    tile_of_row = jnp.arange(row_count, dtype=jnp.int32) // CAND_DEV
    selector = (tile_of_row[:, None] == jnp.arange(hist_count, dtype=jnp.int32)[None, :]).astype(
        jnp.float32
    )
    weights_full = jnp.repeat(jnp.dot(selector, my_mask), BLK, axis=1) * in_history[None, :]

    def compute_heads(unused_arg):
        per_head = []
        for head_num in range(H):
            page_rows = resident[head_num]
            scores = (
                lax.dot_general(
                    piece[:, head_num * DH : (head_num + 1) * DH],
                    page_rows[:, :DH],
                    (((1,), (1,)), ((), ())),
                    preferred_element_type=jnp.float32,
                )
                * score_scale
            )
            weighted = (jax.nn.silu(scores) * weights_full).astype(jnp.bfloat16)
            per_head.append(
                jnp.dot(weighted, page_rows[:, DH:], preferred_element_type=jnp.float32)
            )
        return jnp.concatenate(per_head, axis=1)

    def nothing(unused_arg):
        return jnp.zeros((row_count, D), jnp.float32)

    terms = lax.cond(jnp.any(weights_full > 0), compute_heads, nothing, 0)
    attended = lax.psum_scatter(
        terms.astype(jnp.bfloat16), "hist", scatter_dimension=0, tiled=True
    ).astype(jnp.float32)
    self_scores = (
        jnp.sum(
            (queries.astype(jnp.float32) * cand_keys.astype(jnp.float32)).reshape(CAND_DEV, H, DH),
            axis=2,
        )
        * score_scale
    )
    own_term = (
        jax.nn.silu(self_scores)[:, :, None]
        * cand_values.astype(jnp.float32).reshape(CAND_DEV, H, DH)
    ).reshape(CAND_DEV, D)
    attn_sum = attended + own_term
    centre = attn_sum - jnp.mean(attn_sum, axis=1, keepdims=True)
    variance = jnp.mean(centre * centre, axis=1, keepdims=True)
    mixed = (centre * lax.rsqrt(variance + 1e-05) * norm_gain * gating).astype(jnp.bfloat16)
    result = jnp.dot(mixed, w_out, preferred_element_type=jnp.float32)
    live_rows = position * CAND_DEV + jnp.arange(CAND_DEV, dtype=jnp.int32) < candidate_count[0]
    return jnp.where(live_rows[:, None], result, jnp.zeros_like(result)).astype(jnp.bfloat16)[None]


def solution(mesh):
    return jax.shard_map(
        body,
        mesh=mesh,
        in_specs=(
            P("user", "hist", None),
            P("hist", "user", None, None),
            P("user", "hist", None),
            P("user", "hist"),
            P("user"),
            P("user"),
            P("user", None, None),
            P(),
            P(),
        ),
        out_specs=P("user", "hist", None),
        check_vma=False,
    )
```

profile of v0, /device:TPU:8, one launch (start us, length us, event | category | flops | bytes accessed | tf_op | source)
XLA Modules:
  0.0 326.6 jit_solution(5052606279478672308)
XLA Ops:
  6.5 2.5 fusion.89
  9.0 0.7 slice.321
  9.7 0.0 all-gather.2.cloned.1.call-update
  9.7 0.9 convert_reduce_fusion
  10.6 0.7 add_bitcast_fusion
  11.3 0.7 multiply_add_fusion
  11.9 0.1 select_reduce_fusion
  12.0 0.1 sub.25
  12.1 10.3 %all_to_all.11 = s32[8,1,3]{2,1,0:T(1,128)S(1)} all-to-all(s32[8,1,3]{2,1,0:T(1,128)S(1)} %bitcast.225), channel_id=1, replica_groups=mesh['hist'=32,'user'=8] {'user'}, dimensions={0} | all-to-all | bytes 192 | tf_op jit(solution)/shard_map/all_to_all | solution.py:28
  22.5 0.1 reshape.243
  22.6 6.6 %gather_fusion.2 = bf16[24,512,256]{2,1,0:T(8,128)(2,1)} fusion(bf16[16,512,256]{2,1,0:T(8,128)(2,1)} %bitcast.202, s32[1024]{0:T(1024)S(1)} %pad_clamp_fusion.2), kind=kCustom, calls=%fused_computation.2 | custom fusion | bytes 12583008 | tf_op jit(solution)/shard_map/gather | solution.py:27
  29.2 6.3 %all-to-all-start.1 = ((bf16[8,3,512,256]{3,2,1,0:T(8,128)(2,1)}), bf16[8,3,512,256]{3,2,1,0:T(8,128)(2,1)}, u32[]{:S(2)}, u32[]{:S(2)}) async-start(bf16[8,3,512,256]{3,2,1,0:T(8,128)(2,1)} %bitcast.201), calls=%async_computation.1 | async-start | bytes 12582912 | tf_op jit(solution)/shard_map/all_to_all | solution.py:30
  35.5 0.1 dynamic-slice_convert_fusion
  35.6 0.1 copy.36
  36.4 0.5 fusion.74
  36.8 1.9 fusion.68
  39.4 75.6 %all-to-all-done.1 = bf16[8,3,512,256]{3,2,1,0:T(8,128)(2,1)} async-done(((bf16[8,3,512,256]{3,2,1,0:T(8,128)(2,1)}), bf16[8,3,512,256]{3,2,1,0:T(8,128)(2,1)}, u32[]{:S(2)}, u32[]{:S(2)}) %all-to-all-start.1) | async-done | bytes 6291488 | tf_op jit(solution)/shard_map/all_to_all | solution.py:30
  114.9 4.3 %broadcast_in_dim.24 = f32[2048,2,512]{0,2,1:T(8,128)} broadcast(f32[2048,2]{0,1:T(2,128)S(1)} %fusion.74), dimensions={0,1} | broadcast | bytes 8404992 | tf_op jit(solution)/shard_map/broadcast_in_dim | solution.py:73
  119.2 59.0 %conditional.1 = (bf16[2048,1024]{0,1:T(8,128)(2,1)}) conditional(s32[]{:T(128)} %convert_element_type.115, () %tuple.30, (bf16[8,3,512,256]{3,2,1,0:T(8,128)(2,1)}, s32[16,1]{0,1:T(1,128)S(1)}, s32[]{:T(128)}, s32[16,1]{0,1:T(1,128)S(1)}, s32[]{:T(128)}, /*index=5*/s32[16]{0:T(128)S(1)}, bf16[2048,1024]{1,0:T(8,128)(2,1)}, ...), branch_computations={%region_3.4_spmd, %region_4.5_spmd.clone} | conditional | flops 8724154368 | bytes 192979712 | solution.py:97
  119.2 0.7 gather_fusion
  119.9 5.6 %gather_fusion.1 = bf16[16,512,256]{2,1,0:T(8,128)(2,1)} fusion(bf16[24,512,256]{2,1,0:T(8,128)(2,1)} %bitcast.11, s32[1024]{0:T(1024)S(1)} %pad_clamp_fusion), kind=kCustom, calls=%fused_computation.1 | custom fusion | bytes 8388672 | tf_op jit(solution)/shard_map/gather | solution.py:34
  125.5 2.6 fusion.90
  128.1 5.8 %fusion.32 = bf16[2048,1024]{0,1:T(8,128)(2,1)S(1)} fusion(f32[2048,2,512]{0,2,1:T(8,128)} %get-tuple-element.197, f32[1024]{0:T(1024)S(1)} %bitcast.226, bf16[2048,1024]{1,0:T(8,128)(2,1)} %get-tuple-element.196, bf16[1024,256]{1,0:T(8,128)(2,1)S(1)} %bitcast.223), kind=kOutput, calls=%fused_computation.52 | convolution fusion | flops 553648128 | bytes 13373440 | tf_op jit(solution)/shard_map/cond/branch_1_fun/dot_general | solution.py:80
  134.0 1.6 convolution_dynamic-update-slice_fusion.7
  135.5 4.5 %fusion.33 = bf16[2048,1024]{0,1:T(8,128)(2,1)S(1)} fusion(f32[2048,2,512]{0,2,1:T(8,128)S(1)} %bitcast.204, f32[1024]{0:T(1024)S(1)} %bitcast.227, bf16[2048,1024]{1,0:T(8,128)(2,1)} %get-tuple-element.196, bf16[1024,256]{1,0:T(8,128)(2,1)S(1)} %bitcast.220), kind=kOutput, calls=%fused_computation.53 | convolution fusion | flops 553648128 | bytes 13373440 | tf_op jit(solution)/shard_map/cond/branch_1_fun/dot_general | solution.py:80
  140.0 1.6 convolution_dynamic-update-slice_fusion.6
  141.6 4.5 %fusion.34 = bf16[2048,1024]{0,1:T(8,128)(2,1)S(1)} fusion(f32[2048,2,512]{0,2,1:T(8,128)S(1)} %bitcast.204, f32[1024]{0:T(1024)S(1)} %bitcast.228, bf16[2048,1024]{1,0:T(8,128)(2,1)} %get-tuple-element.196, bf16[1024,256]{1,0:T(8,128)(2,1)S(1)} %bitcast.218), kind=kOutput, calls=%fused_computation.54 | convolution fusion | flops 553648128 | bytes 13373440 | tf_op jit(solution)/shard_map/cond/branch_1_fun/dot_general | solution.py:80
  146.1 1.6 convolution_dynamic-update-slice_fusion.5
  147.6 4.5 %fusion.35 = bf16[2048,1024]{0,1:T(8,128)(2,1)S(1)} fusion(f32[2048,2,512]{0,2,1:T(8,128)S(1)} %bitcast.204, f32[1024]{0:T(1024)S(1)} %bitcast.229, bf16[2048,1024]{1,0:T(8,128)(2,1)} %get-tuple-element.196, bf16[1024,256]{1,0:T(8,128)(2,1)S(1)} %bitcast.216), kind=kOutput, calls=%fused_computation.55 | convolution fusion | flops 553648128 | bytes 13373440 | tf_op jit(solution)/shard_map/cond/branch_1_fun/dot_general | solution.py:80
  152.1 1.6 convolution_dynamic-update-slice_fusion.4
  153.7 4.7 %fusion.36 = bf16[2048,1024]{0,1:T(8,128)(2,1)S(1)} fusion(f32[2048,2,512]{0,2,1:T(8,128)S(1)} %bitcast.204, f32[1024]{0:T(1024)S(1)} %bitcast.230, bf16[2048,1024]{1,0:T(8,128)(2,1)} %get-tuple-element.196, bf16[1024,256]{1,0:T(8,128)(2,1)S(1)} %bitcast.214), kind=kOutput, calls=%fused_computation.56 | convolution fusion | flops 553648128 | bytes 13373440 | tf_op jit(solution)/shard_map/cond/branch_1_fun/dot_general | solution.py:80
  158.4 1.6 convolution_dynamic-update-slice_fusion.3
  160.0 4.5 %fusion.37 = bf16[2048,1024]{0,1:T(8,128)(2,1)S(1)} fusion(f32[2048,2,512]{0,2,1:T(8,128)S(1)} %bitcast.204, f32[1024]{0:T(1024)S(1)} %bitcast.231, bf16[2048,1024]{1,0:T(8,128)(2,1)} %get-tuple-element.196, bf16[1024,256]{1,0:T(8,128)(2,1)S(1)} %bitcast.212), kind=kOutput, calls=%fused_computation.57 | convolution fusion | flops 553648128 | bytes 13373440 | tf_op jit(solution)/shard_map/cond/branch_1_fun/dot_general | solution.py:80
  164.4 1.6 convolution_dynamic-update-slice_fusion.2
  166.0 4.5 %fusion.38 = bf16[2048,1024]{0,1:T(8,128)(2,1)S(1)} fusion(f32[2048,2,512]{0,2,1:T(8,128)S(1)} %bitcast.204, f32[1024]{0:T(1024)S(1)} %bitcast.232, bf16[2048,1024]{1,0:T(8,128)(2,1)} %get-tuple-element.196, bf16[1024,256]{1,0:T(8,128)(2,1)S(1)} %bitcast.210), kind=kOutput, calls=%fused_computation.58 | convolution fusion | flops 553648128 | bytes 13373440 | tf_op jit(solution)/shard_map/cond/branch_1_fun/dot_general | solution.py:80
  170.5 1.6 convolution_dynamic-update-slice_fusion.1
  172.1 4.5 %fusion.39 = bf16[2048,1024]{0,1:T(8,128)(2,1)S(1)} fusion(f32[2048,2,512]{0,2,1:T(8,128)S(1)} %bitcast.204, f32[1024]{0:T(1024)S(1)} %bitcast.233, bf16[2048,1024]{1,0:T(8,128)(2,1)} %get-tuple-element.196, bf16[1024,256]{1,0:T(8,128)(2,1)S(1)} %bitcast.208), kind=kOutput, calls=%fused_computation.59 | convolution fusion | flops 553648128 | bytes 13373440 | tf_op jit(solution)/shard_map/cond/branch_1_fun/dot_general | solution.py:80
  176.6 1.6 convolution_dynamic-update-slice_fusion
  178.2 6.4 %copy.31 = bf16[2048,1024]{1,0:T(8,128)(2,1)} copy(bf16[2048,1024]{0,1:T(8,128)(2,1)} %get-tuple-element.240) | data formatting | bytes 8388608
  184.6 0.0 reduce-scatter.4.cloned.1.call-update
  184.7 0.1 reduce_sum.47
  184.8 0.1 copy.29
  184.9 0.1 copy.30
  185.7 129.5 %reduce-scatter.4.cloned.1.call-done = bf16[64,1024]{1,0:T(8,128)(2,1)} async-done(((bf16[2048,1024]{1,0:T(8,128)(2,1)}), bf16[64,1024]{1,0:T(8,128)(2,1)}) %reduce-scatter.4.cloned.1.call-update) | async-done | bytes 131088 | tf_op jit(solution)/shard_map/reduce_scatter | solution.py:98
  315.2 0.1 mul.319
  315.3 1.1 fusion.88
  316.4 1.1 multiply_reduce_fusion
  317.6 2.2 fusion.70
  (31 shorter events, 0.2 us)
Async XLA Ops:
  6.5 311.0 %copy-start = (bf16[1024,1024]{1,0:T(8,128)(2,1)S(1)}, bf16[1024,1024]{1,0:T(8,128)(2,1)}, u32[]{:S(2)}) copy-start(bf16[1024,1024]{1,0:T(8,128)(2,1)} %param.19) | copy-start | bytes 6291460
  6.5 108.4 %all-gather.2.cloned.1.call-start = ((), (), s32[]{:S(2)}) async-start(), calls=%async_computation.3 | async-start | bytes 4325376 | tf_op jit(solution)/shard_map/all_gather | solution.py:67
  29.2 6.3 %copy-start.1 = (s32[1,32,64]{2,1,0:T(8,128)S(1)}, s32[1,32,64]{2,1,0:T(8,128)}, u32[]{:S(2)}) copy-start(s32[1,32,64]{2,1,0:T(8,128)} %param.17) | copy-start | bytes 24580
  29.2 85.7 %all-to-all-start.1 = ((bf16[8,3,512,256]{3,2,1,0:T(8,128)(2,1)}), bf16[8,3,512,256]{3,2,1,0:T(8,128)(2,1)}, u32[]{:S(2)}, u32[]{:S(2)}) async-start(bf16[8,3,512,256]{3,2,1,0:T(8,128)(2,1)} %bitcast.201), calls=%async_computation.1 | async-start | bytes 12582912 | tf_op jit(solution)/shard_map/all_to_all | solution.py:30
  35.5 279.7 %reduce-scatter.4.cloned.1.call-start = ((), (), s32[]{:S(2)}) async-start(), calls=%async_computation.4 | async-start | bytes 4325376 | tf_op jit(solution)/shard_map/reduce_scatter | solution.py:98
  125.5 10.0 %slice-start = ((s8[8388608]{0:T(1024)(128)(4,1)}), s8[4194304]{0:T(1024)(128)(4,1)S(1)}, s32[]{:S(2)}) async-start(s8[8388608]{0:T(1024)(128)(4,1)} %bitcast.203), calls=%async_computation.5 | async-start | bytes 8388608 | tf_op jit(solution)/shard_map/cond
  128.1 7.4 %slice-start.1 = ((s8[8388608]{0:T(1024)(128)(4,1)}), s8[4194304]{0:T(1024)(128)(4,1)S(1)}, s32[]{:S(2)}) async-start(s8[8388608]{0:T(1024)(128)(4,1)} %bitcast.203), calls=%async_computation.6 | async-start | bytes 8388608 | tf_op jit(solution)/shard_map/cond
  178.2 139.4 %copy-start.2 = (f32[1024]{0:T(1024)S(1)}, f32[1024]{0:T(1024)}, u32[]{:S(2)}) copy-start(f32[1024]{0:T(1024)} %param.18) | copy-start | bytes 12292
Sparse Core Ops, SparseCore 0:
  10.1 100.8 all-gather.1
  184.7 130.4 reduce-scatter.3
where the time goes:
time: 328 us; the launch traced here: 327 us
  waiting for transfers between devices  205 us (62%)
  matrix products  52.6 us (16%)
  local copies, waits for them, and re-layouts  27.4 us (8%)
  between operations  15.5 us (5%)
  blocking collectives  10.3 us (3%)
  other arithmetic  9.25 us (3%)
  starting transfers between devices  6.29 us (2%)
    reduce_scatter x1, waiting for transfers between devices, body(): lax.psum_scatter(terms.astype(jnp.bfloat16), 'hist', scatter_dimension=0,...  130 us
    all_to_all x1, waiting for transfers between devices, fetch_pages(): lax.all_to_all(located, 'user', split_axis=0, concat_axis=0, tiled=True)  75.6 us
    dot_general x8, matrix products, compute_heads(): lax.dot_general(piece[:, head_num * DH:(head_num + 1) * DH], page_rows[:,...  37.4 us
    dot_general x8, matrix products, compute_heads(): jnp.dot(weighted, page_rows[:, DH:], preferred_element_type=jnp.float32)  12.6 us
    all_to_all x1, blocking collectives, fetch_pages(): lax.all_to_all(wanted, 'user', split_axis=0, concat_axis=0, tiled=True)  10.3 us
    gather x1, local copies, waits for them, and re-layouts, fetch_pages(): stored_pages[jnp.maximum(lax.all_to_all(wanted, 'user', split_axis=0, con...  6.64 us
    unnamed x9, local copies, waits for them, and re-layouts  6.56 us
  transfers between devices with their start and end apart: 3, of which 2 were waited for; matrix products, arithmetic and copies ran while one was open for 4% of the time, Pallas kernels for 0%

commit v1 on v0

v1 whole, which is shorter than its diff:
```python
import jax
import jax.numpy as jnp
from jax import lax
from jax.experimental import pallas as pl
from jax.experimental.pallas import tpu as pltpu
from jax.sharding import PartitionSpec as P

D = 1024
H = 8
DH = 128
BLK = 512
TILE = 64
NY = 4
NZ = 8
PEERS = 8
CAP = 3
PAGES = 16
SLOTS = PEERS * CAP
LAG = 2
SCALE = DH ** (-0.5)
MESH = pl.DeviceIdType.MESH


def silu(v):
    half = v * 0.5
    return half * jnp.tanh(half) + half


def kernel(
    length_ref,
    count_ref,
    bmask,
    proj,
    owner_col,
    owner_row,
    page_col,
    gain,
    cache,
    w_out,
    result,
    cache_v,
    w_v,
    stage,
    pages,
    queries,
    partial,
    gating,
    own_term,
    msg,
    asked,
    msg_s,
    asked_s,
    rs_send,
    rs_recv,
    xs_send,
    xs_recv,
    local_sem,
    req_send,
    req_recv,
    page_send,
    page_recv,
    pair_send,
    pair_recv,
    info_sem,
    ag_send,
    ag_recv,
    sum_send,
    sum_recv,
    x_sem,
):
    hist, user = lax.axis_index("hist"), lax.axis_index("user")
    xh, z, core = hist // 16, (hist // 2) % NZ, hist % 2
    xl, y = user // NY, user % NY

    def at(xh_, z_, core_):
        return (xh_ * 16 + z_ * 2 + core_, user)

    up, down = at(xh, (z + 1) % NZ, core), at(xh, (z + 7) % NZ, core)
    across, pair = at(1 - xh, z, core), at(xh, z, 1 - core)

    def owner_at(d):
        return (hist, ((xl + d // NY) % 2) * NY + (y + d % NY) % NY)

    def asker_at(d):
        return (hist, ((xl + d // NY) % 2) * NY + (y + NY - d % NY) % NY)

    def remote(src, dst, send, recv, device):
        return pltpu.make_async_remote_copy(
            src_ref=src, dst_ref=dst, send_sem=send, recv_sem=recv, device_id=device, device_id_type=MESH
        )

    load_cache = pltpu.make_async_copy(cache, cache_v, local_sem.at[0])
    load_cache.start()
    load_w = pltpu.make_async_copy(w_out, w_v, local_sem.at[1])
    load_w.start()

    barrier = pltpu.get_barrier_semaphore()
    for d in range(1, PEERS):
        pl.semaphore_signal(barrier, inc=1, device_id=asker_at(d), device_id_type=MESH)
    for device in (up, down, across, pair):
        pl.semaphore_signal(barrier, inc=1, device_id=device, device_id_type=MESH)

    row = lax.broadcasted_iota(jnp.int32, (16, 128), 0)
    lane = lax.broadcasted_iota(jnp.int32, (16, 128), 1)
    owners = jnp.broadcast_to(owner_col[...], (16, 128))
    same = (owners == jnp.broadcast_to(owner_row[...], (16, 128))) & (lane < row)
    rank = jnp.minimum(jnp.sum(same.astype(jnp.int32), axis=1, keepdims=True), CAP - 1)
    place = (((owners >> 2) ^ xl) & 1) * NY + ((owners - y) & 3)
    slot = jnp.broadcast_to(rank, (16, 128)) * PEERS + place
    match = slot == lane
    want = jnp.broadcast_to(page_col[...], (16, 128))
    valid = jnp.clip(length_ref[0] - (hist * 2 + (row >> 3)) * BLK, 0, BLK)
    zero = jnp.zeros((16, 128), jnp.int32)

    def pick(values):
        return jnp.sum(jnp.where(match, values, zero), axis=0, keepdims=True)

    r8 = lax.broadcasted_iota(jnp.int32, (8, 128), 0)
    wanted = jnp.clip(pick(want), 0, PAGES - 1)
    heads = jnp.clip(pick(row & 7), 0, H - 1)
    first = jnp.where(r8 == 0, wanted, jnp.where(r8 == 1, heads, pick(valid)))
    msg[0, 0:8, :] = first
    msg[0, 8:24, :] = slot

    for e in range(H):
        q = silu(proj[:, 2 * D + e * DH : 2 * D + (e + 1) * DH].astype(jnp.float32))
        queries[z, xh, e] = q.astype(jnp.bfloat16)

    pl.semaphore_wait(barrier, PEERS - 1 + 4)

    ask = []
    for d in range(1, PEERS):
        ask.append(remote(msg.at[0, 0:8], asked.at[d], req_send.at[d], req_recv.at[d], owner_at(d)))
    for copy in ask:
        copy.start()
    ag_x = remote(queries.at[z, xh], queries.at[z, xh], ag_send.at[0, 4], ag_recv.at[0, 4], across)
    ag_x.start()
    tell = remote(msg.at[0], msg.at[1], info_sem.at[0], info_sem.at[1], pair)
    tell.start()
    load_cache.wait()
    for copy in ask:
        copy.wait_recv()
    copy_asked = pltpu.make_async_copy(asked.at[pl.ds(1, PEERS - 1)], asked_s.at[pl.ds(1, PEERS - 1)], local_sem.at[2])
    copy_asked.start()
    tell.wait()
    copy_msg = pltpu.make_async_copy(msg, msg_s, local_sem.at[3])
    copy_msg.start()
    copy_asked.wait()
    copy_msg.wait()

    def page_copy(k, d):
        i = k * PEERS + d
        return remote(stage.at[i], pages.at[0, i], page_send.at[i], page_recv.at[i], asker_at(d))

    def serve(k, carry):
        for d in (4, 1, 3, 5, 7, 2, 6):
            stage[k * PEERS + d] = cache_v[asked_s[d, 0, k * PEERS + d]]
            page_copy(k, d).start()
        pages[0, k * PEERS] = cache_v[msg_s[0, 0, k * PEERS]]
        return carry

    lax.fori_loop(0, CAP, serve, 0)

    ag_x.wait()

    def gather_step(s):
        zu, zd = (z + NZ - s) % NZ, (z + s) % NZ
        if s < 3:
            up_part, down_part = queries.at[zu], queries.at[zd]
        else:
            up_part, down_part = queries.at[zu, 0], queries.at[zd, 1]
        return (
            remote(up_part, up_part, ag_send.at[0, s], ag_recv.at[0, s], up),
            remote(down_part, down_part, ag_send.at[1, s], ag_recv.at[1, s], down),
        )

    steps = [gather_step(s) for s in range(4)]
    for copy in steps[0]:
        copy.start()

    gating[...] = silu(proj[:, 0:D].astype(jnp.float32))
    for e in range(H):
        cols = slice(e * DH, (e + 1) * DH)
        v = silu(proj[:, D + e * DH : D + (e + 1) * DH].astype(jnp.float32)).astype(jnp.bfloat16)
        k = silu(proj[:, 3 * D + e * DH : 3 * D + (e + 1) * DH].astype(jnp.float32)).astype(jnp.bfloat16)
        q = queries[z, xh, e]
        score = jnp.sum(q.astype(jnp.float32) * k.astype(jnp.float32), axis=1, keepdims=True) * SCALE
        own_term[:, cols] = silu(score) * v.astype(jnp.float32)

    for s in range(4):
        for direction in range(2):
            steps[s][direction].wait_recv()
            if s < 3:
                steps[s + 1][direction].start()

    def pair_copy(i):
        return remote(pages.at[0, i], pages.at[1, i], pair_send.at[i], pair_recv.at[i], pair)

    rows = lax.broadcasted_iota(jnp.int32, (BLK, DH), 0)
    chunk = 512

    def attend(t, carry):
        side = t % 2
        i = t // 2 - side * LAG

        @pl.when((i >= 0) & (i < SLOTS))
        def _():
            @pl.when((side == 0) & (i % PEERS != 0))
            def _():
                page_copy(0, i).wait_recv()

            @pl.when(side == 0)
            def _():
                pair_copy(i).start()

            @pl.when(side == 1)
            def _():
                pair_copy(i).wait_recv()

            head = msg_s[side, 1, i]
            live = msg_s[side, 2, i]
            k = pages[side, i, :, 0:DH]
            v = pages[side, i, :, DH : 2 * DH]
            v = jnp.where(rows < live, v, jnp.zeros_like(v))
            n = chunk // 128
            for j in range(1024 // chunk):
                q = queries[j * n : (j + 1) * n, :, head].reshape(chunk, DH)
                score = lax.dot_general(q, k, (((1,), (1,)), ((), ())), preferred_element_type=jnp.float32)
                half = score * (SCALE * 0.5)
                weight = (half * jnp.tanh(half) + half).astype(jnp.bfloat16)
                term = jnp.dot(weight, v, preferred_element_type=jnp.float32)
                partial[side, i, j * chunk : (j + 1) * chunk, :] = term.astype(jnp.bfloat16)

        return carry

    lax.fori_loop(0, 2 * (SLOTS + LAG), attend, 0)

    def term_of(zd, xd, e):
        total = None
        tile = xd * 16 + zd * 2 + core
        for side in range(2):
            other = core if side == 0 else 1 - core
            for b in range(2):
                block = (hist - core + other) * 2 + b
                m = bmask[tile, block].astype(jnp.float32)
                s = msg_s[side, 8 + b * H + e, 0]
                part = partial[side, s, pl.ds(pl.multiple_of(zd * 128 + xd * 64, 64), TILE), :]
                part = part.astype(jnp.float32) * m
                total = part if total is None else total + part
        return total

    def sum_copy(g, s, j):
        return remote(
            rs_send.at[g, s, j], rs_recv.at[g, s, j], sum_send.at[g, s, j], sum_recv.at[g, s, j], up if g == 0 else down
        )

    def ring_step(s, arrived):
        for j in range(2):
            for g in range(2):
                zd = (z + NZ - 1 - s) % NZ if g == 0 else (z + 1 + s) % NZ
                terms = [term_of(zd, j, g * 4 + e) for e in range(4)]
                if arrived:
                    sum_copy(g, s - 1, j).wait_recv()
                for e in range(4):
                    cols = slice(e * DH, (e + 1) * DH)
                    v = terms[e]
                    if arrived:
                        v = v + rs_recv[g, s - 1, j, :, cols].astype(jnp.float32)
                    rs_send[g, s, j, :, cols] = v.astype(jnp.bfloat16)
                sum_copy(g, s, j).start()

    ring_step(0, False)

    def ring_body(s, carry):
        ring_step(s, True)
        return carry

    lax.fori_loop(1, NZ - 1, ring_body, 0)
    load_w.wait()
    for j in range(2):
        for g in range(2):
            sum_copy(g, NZ - 2, j).wait_recv()

    def final_terms(xd):
        out = []
        for e in range(H):
            g, cols = e // 4, slice(e % 4 * DH, (e % 4 + 1) * DH)
            out.append(term_of(z, xd, e) + rs_recv[g, NZ - 2, xd, :, cols].astype(jnp.float32))
        return out

    for e, v in enumerate(final_terms(1 - xh)):
        xs_send[:, e * DH : (e + 1) * DH] = v.astype(jnp.bfloat16)
    x_copy = remote(xs_send, xs_recv, x_sem.at[0], x_sem.at[1], across)
    x_copy.start()
    for e, v in enumerate(final_terms(xh)):
        cols = slice(e * DH, (e + 1) * DH)
        own_term[:, cols] = own_term[:, cols] + v
    x_copy.wait()
    attn = own_term[...] + xs_recv[...].astype(jnp.float32)
    centre = attn - jnp.mean(attn, axis=1, keepdims=True)
    variance = jnp.mean(centre * centre, axis=1, keepdims=True)
    mixed = (centre * lax.rsqrt(variance + 1e-05) * gain[...] * gating[...]).astype(jnp.bfloat16)
    out = jnp.dot(mixed, w_v[...], preferred_element_type=jnp.float32)
    live_row = hist * TILE + lax.broadcasted_iota(jnp.int32, (TILE, D), 0) < count_ref[0]
    result[...] = jnp.where(live_row, out, jnp.zeros_like(out)).astype(jnp.bfloat16)

    for copy in ask:
        copy.wait_send()
    for s in range(4):
        for direction in range(2):
            steps[s][direction].wait_send()

    def drain_pages(k, carry):
        for d in range(PEERS):
            if d:
                page_copy(k, d).wait_send()
            pair_copy(k * PEERS + d).wait_send()
        return carry

    lax.fori_loop(0, CAP, drain_pages, 0)

    def drain_sums(s, carry):
        for g in range(2):
            for j in range(2):
                sum_copy(g, s, j).wait_send()
        return carry

    lax.fori_loop(0, NZ - 1, drain_sums, 0)


def body(proj, cache, owner, page, length, count, bmask, gain, w_out):
    vmem, smem = pl.BlockSpec(memory_space=pltpu.VMEM), pl.BlockSpec(memory_space=pltpu.SMEM)
    anywhere = pl.BlockSpec(memory_space=pl.ANY)
    owner_col = owner[0]
    owner_row = jnp.pad(owner.reshape(1, 16), ((0, 0), (0, 112)), constant_values=-1)
    page_col = page.reshape(16, 1)
    dma = pltpu.SemaphoreType.DMA
    bf, f32, i32 = jnp.bfloat16, jnp.float32, jnp.int32
    out = pl.pallas_call(
        kernel,
        out_shape=jax.ShapeDtypeStruct((TILE, D), bf),
        in_specs=[smem, smem, smem, vmem, vmem, vmem, vmem, vmem, anywhere, anywhere],
        out_specs=vmem,
        scratch_shapes=[
            pltpu.VMEM((16, BLK, 2 * DH), bf),
            pltpu.VMEM((D, D), bf),
            pltpu.VMEM((SLOTS, BLK, 2 * DH), bf),
            pltpu.VMEM((2, SLOTS, BLK, 2 * DH), bf),
            pltpu.VMEM((NZ, 2, H, TILE, DH), bf),
            pltpu.VMEM((2, SLOTS, 1024, DH), bf),
            pltpu.VMEM((TILE, D), f32),
            pltpu.VMEM((TILE, D), f32),
            pltpu.VMEM((2, 24, 128), i32),
            pltpu.VMEM((PEERS, 8, 128), i32),
            pltpu.SMEM((2, 24, 128), i32),
            pltpu.SMEM((PEERS, 8, 128), i32),
            pltpu.VMEM((2, NZ - 1, 2, TILE, D // 2), bf),
            pltpu.VMEM((2, NZ - 1, 2, TILE, D // 2), bf),
            pltpu.VMEM((TILE, D), bf),
            pltpu.VMEM((TILE, D), bf),
            dma((4,)),
            dma((PEERS,)),
            dma((PEERS,)),
            dma((SLOTS,)),
            dma((SLOTS,)),
            dma((SLOTS,)),
            dma((SLOTS,)),
            dma((2,)),
            dma((2, 5)),
            dma((2, 5)),
            dma((2, NZ - 1, 2)),
            dma((2, NZ - 1, 2)),
            dma((2,)),
        ],
        compiler_params=pltpu.CompilerParams(
            collective_id=0, has_side_effects=True, vmem_limit_bytes=60 * 1024 * 1024
        ),
        name="score_candidates",
    )(length, count, bmask[0], proj[0], owner_col, owner_row, page_col, gain.reshape(1, D), cache[0], w_out)
    return out[None]


def solution(mesh):
    return jax.shard_map(
        body,
        mesh=mesh,
        in_specs=(
            P("user", "hist", None),
            P("hist", "user", None, None),
            P("user", "hist", None),
            P("user", "hist"),
            P("user"),
            P("user"),
            P("user", None, None),
            P(),
            P(),
        ),
        out_specs=P("user", "hist", None),
        check_vma=False,
    )
```

time: 328 us -> 133 us (0.41)
  waiting for transfers between devices: 205 us -> 0 us
  Pallas kernels: 0 us -> 126 us
  matrix products: 52.6 us -> 0 us
  local copies, waits for them, and re-layouts: 27.4 us -> 5.46 us
  between operations: 15.5 us -> 1.31 us
  blocking collectives: 10.3 us -> 0 us
  other arithmetic: 9.25 us -> 0 us
  starting transfers between devices: 6.29 us -> 0 us
    reduce_scatter x1 -> x0, waiting for transfers between devices: 130 us -> none  [body(): lax.psum_scatter(terms.astype(jnp.bfloat16), 'hist', scatter_dimension=0,...]
    pallas_call x0 -> x1, Pallas kernels: none -> 126 us  [body(): pl.pallas_call(kernel, out_shape=jax.ShapeDtypeStruct((TILE, D), bf), in_...]
    all_to_all x1 -> x0, waiting for transfers between devices: 75.6 us -> none  [fetch_pages(): lax.all_to_all(located, 'user', split_axis=0, concat_axis=0, tiled=True)]
    dot_general x18 -> x0, matrix products: 52.6 us -> none  [the longest x8 37.4 us: compute_heads(): lax.dot_general(piece[:, head_num * DH:(head_num + 1) * DH], page_rows[:,...]
    gather x3 -> x0, local copies, waits for them, and re-layouts: 12.9 us -> none  [the longest x1 6.64 us: fetch_pages(): stored_pages[jnp.maximum(lax.all_to_all(wanted, 'user', split_axis=0, con...]
    all_to_all x1 -> x0, blocking collectives: 10.3 us -> none  [fetch_pages(): lax.all_to_all(wanted, 'user', split_axis=0, concat_axis=0, tiled=True)]
    all_to_all x1 -> x0, starting transfers between devices: 6.29 us -> none  [fetch_pages(): lax.all_to_all(located, 'user', split_axis=0, concat_axis=0, tiled=True)]
    unnamed x9 -> x1, local copies, waits for them, and re-layouts: 6.56 us -> 1.57 us
  transfers between devices with their start and end apart: 3 -> 0, of which waited for: 2 -> 0; matrix products, arithmetic and copies ran while one was open for 4% -> 0% of each run, Pallas kernels for 0% -> 0%
where the time goes in v1:
time: 133 us
  Pallas kernels  126 us (95%)
  local copies, waits for them, and re-layouts  5.46 us (4%)
    pallas_call x1, Pallas kernels, body(): pl.pallas_call(kernel, out_shape=jax.ShapeDtypeStruct((TILE, D), bf), in_...  126 us

profile of v1, /device:TPU:8, one launch (start us, length us, event | category | flops | bytes accessed | tf_op | source)
XLA Modules:
  0.0 133.1 jit_solution(1851462592369558503)
XLA Ops:
  1.3 1.2 pad.4.owner_row
  2.5 1.3 copy.11.page_col
  3.9 1.3 copy.10.owner_col
  5.2 126.3 %score_candidates.1 = bf16[64,1024]{1,0:T(8,128)(2,1)} custom-call(s32[1]{0:T(128)S(6)} %copy.13.length_ref, s32[1]{0:T(128)S(6)} %copy.14.count_ref, s32[32,64]{1,0:T(8,128)} %bitcast.11, bf16[64,4096]{1,0:T(8,128)(2,1)} %bitcast.10, s32[16,1]{1,0:T(8,128)} %copy.10.owner_col, s32[1,128]{1,0:T(1,128)} %pad.4.owner_row, s32[16,1]{1,0:T(8,128)} %copy.11.page_col, ...), custom_call_target="tpu_custom_call" | custom-call | tf_op jit(solution)/shard_map/score_candidates/pallas_call | solution.py:339
  131.5 1.6 %copy.15 = bf16[1,64,1024]{2,1,0:T(8,128)(2,1)} copy(bf16[1,64,1024]{2,1,0:T(8,128)(2,1)} %bitcast.9) | data formatting | bytes 262144

commit v2 on v1

--- a/solution.py
+++ b/solution.py
@@ -27,17 +27,21 @@
 
 
 def kernel(
+    length_hbm,
+    count_hbm,
+    owner_ref,
+    page_ref,
+    gain,
+    bmask_hbm,
+    proj_hbm,
+    cache,
+    w_out,
+    result,
     length_ref,
     count_ref,
     bmask,
+    seen,
     proj,
-    owner_col,
-    owner_row,
-    page_col,
-    gain,
-    cache,
-    w_out,
-    result,
     cache_v,
     w_v,
     stage,
@@ -50,10 +54,14 @@
     asked,
     msg_s,
     asked_s,
-    rs_send,
-    rs_recv,
-    xs_send,
-    xs_recv,
+    za_send,
+    za_recv,
+    zb_send,
+    zb_recv,
+    xb_send,
+    xb_recv,
+    xa_send,
+    xa_recv,
     local_sem,
     req_send,
     req_recv,
@@ -64,9 +72,13 @@
     info_sem,
     ag_send,
     ag_recv,
-    sum_send,
-    sum_recv,
-    x_sem,
+    za_ssem,
+    za_rsem,
+    zb_ssem,
+    zb_rsem,
+    xb_ssem,
+    xb_rsem,
+    xa_sem,
 ):
     hist, user = lax.axis_index("hist"), lax.axis_index("user")
     xh, z, core = hist // 16, (hist // 2) % NZ, hist % 2
@@ -89,8 +101,16 @@
             src_ref=src, dst_ref=dst, send_sem=send, recv_sem=recv, device_id=device, device_id_type=MESH
         )
 
+    load_length = pltpu.make_async_copy(length_hbm, length_ref, local_sem.at[6])
+    load_length.start()
+    load_count = pltpu.make_async_copy(count_hbm, count_ref, local_sem.at[7])
+    load_count.start()
     load_cache = pltpu.make_async_copy(cache, cache_v, local_sem.at[0])
     load_cache.start()
+    load_proj = pltpu.make_async_copy(proj_hbm, proj, local_sem.at[4])
+    load_proj.start()
+    load_mask = pltpu.make_async_copy(bmask_hbm, bmask, local_sem.at[5])
+    load_mask.start()
     load_w = pltpu.make_async_copy(w_out, w_v, local_sem.at[1])
     load_w.start()
 
@@ -102,15 +122,19 @@
 
     row = lax.broadcasted_iota(jnp.int32, (16, 128), 0)
     lane = lax.broadcasted_iota(jnp.int32, (16, 128), 1)
-    owners = jnp.broadcast_to(owner_col[...], (16, 128))
-    same = (owners == jnp.broadcast_to(owner_row[...], (16, 128))) & (lane < row)
+    zero = jnp.zeros((16, 128), jnp.int32)
+    owners, owners_across, want = zero, zero - 1, zero
+    for r in range(16):
+        owners = jnp.where(row == r, owner_ref[0, r], owners)
+        owners_across = jnp.where(lane == r, owner_ref[0, r], owners_across)
+        want = jnp.where(row == r, page_ref[0, r], want)
+    same = (owners == owners_across) & (lane < row)
     rank = jnp.minimum(jnp.sum(same.astype(jnp.int32), axis=1, keepdims=True), CAP - 1)
     place = (((owners >> 2) ^ xl) & 1) * NY + ((owners - y) & 3)
     slot = jnp.broadcast_to(rank, (16, 128)) * PEERS + place
     match = slot == lane
-    want = jnp.broadcast_to(page_col[...], (16, 128))
+    load_length.wait()
     valid = jnp.clip(length_ref[0] - (hist * 2 + (row >> 3)) * BLK, 0, BLK)
-    zero = jnp.zeros((16, 128), jnp.int32)
 
     def pick(values):
         return jnp.sum(jnp.where(match, values, zero), axis=0, keepdims=True)
@@ -118,13 +142,10 @@
     r8 = lax.broadcasted_iota(jnp.int32, (8, 128), 0)
     wanted = jnp.clip(pick(want), 0, PAGES - 1)
     heads = jnp.clip(pick(row & 7), 0, H - 1)
-    first = jnp.where(r8 == 0, wanted, jnp.where(r8 == 1, heads, pick(valid)))
+    blocks = jnp.clip(pick(row >> 3), 0, 1)
+    first = jnp.where(r8 == 0, wanted, jnp.where(r8 == 1, heads, jnp.where(r8 == 2, pick(valid), blocks)))
     msg[0, 0:8, :] = first
     msg[0, 8:24, :] = slot
-
-    for e in range(H):
-        q = silu(proj[:, 2 * D + e * DH : 2 * D + (e + 1) * DH].astype(jnp.float32))
-        queries[z, xh, e] = q.astype(jnp.bfloat16)
 
     pl.semaphore_wait(barrier, PEERS - 1 + 4)
 
@@ -133,20 +154,21 @@
         ask.append(remote(msg.at[0, 0:8], asked.at[d], req_send.at[d], req_recv.at[d], owner_at(d)))
     for copy in ask:
         copy.start()
+    tell = remote(msg.at[0], msg.at[1], info_sem.at[0], info_sem.at[1], pair)
+    tell.start()
+    load_proj.wait()
+    for e in range(H):
+        q = silu(proj[:, 2 * D + e * DH : 2 * D + (e + 1) * DH].astype(jnp.float32))
+        queries[z, xh, e] = q.astype(jnp.bfloat16)
+
     ag_x = remote(queries.at[z, xh], queries.at[z, xh], ag_send.at[0, 4], ag_recv.at[0, 4], across)
     ag_x.start()
-    tell = remote(msg.at[0], msg.at[1], info_sem.at[0], info_sem.at[1], pair)
-    tell.start()
-    load_cache.wait()
     for copy in ask:
         copy.wait_recv()
     copy_asked = pltpu.make_async_copy(asked.at[pl.ds(1, PEERS - 1)], asked_s.at[pl.ds(1, PEERS - 1)], local_sem.at[2])
     copy_asked.start()
-    tell.wait()
-    copy_msg = pltpu.make_async_copy(msg, msg_s, local_sem.at[3])
-    copy_msg.start()
+    load_cache.wait()
     copy_asked.wait()
-    copy_msg.wait()
 
     def page_copy(k, d):
         i = k * PEERS + d
@@ -156,10 +178,12 @@
         for d in (4, 1, 3, 5, 7, 2, 6):
             stage[k * PEERS + d] = cache_v[asked_s[d, 0, k * PEERS + d]]
             page_copy(k, d).start()
-        pages[0, k * PEERS] = cache_v[msg_s[0, 0, k * PEERS]]
         return carry
 
     lax.fori_loop(0, CAP, serve, 0)
+    tell.wait()
+    copy_msg = pltpu.make_async_copy(msg, msg_s, local_sem.at[3])
+    copy_msg.start()
 
     ag_x.wait()
 
@@ -187,6 +211,22 @@
         score = jnp.sum(q.astype(jnp.float32) * k.astype(jnp.float32), axis=1, keepdims=True) * SCALE
         own_term[:, cols] = silu(score) * v.astype(jnp.float32)
 
+    load_mask.wait()
+
+    def see(n, carry):
+        zd, xd = n // 2, n % 2
+        for side in range(2):
+            for b in range(2):
+                other = core if side == 0 else 1 - core
+                m = bmask[xd * 16 + zd * 2 + core, (hist - core + other) * 2 + b].astype(jnp.float32)
+                seen[side, b, pl.ds(pl.multiple_of(n * TILE, TILE), TILE), :] = jnp.full((TILE, DH), m, jnp.float32)
+        return carry
+
+    lax.fori_loop(0, 2 * NZ, see, 0)
+    copy_msg.wait()
+    for k in range(CAP):
+        pages[0, k * PEERS] = cache_v[msg_s[0, 0, k * PEERS]]
+
     for s in range(4):
         for direction in range(2):
             steps[s][direction].wait_recv()
@@ -219,6 +259,7 @@
 
             head = msg_s[side, 1, i]
             live = msg_s[side, 2, i]
+            block = msg_s[side, 3, i]
             k = pages[side, i, :, 0:DH]
             v = pages[side, i, :, DH : 2 * DH]
             v = jnp.where(rows < live, v, jnp.zeros_like(v))
@@ -229,7 +270,8 @@
                 half = score * (SCALE * 0.5)
                 weight = (half * jnp.tanh(half) + half).astype(jnp.bfloat16)
                 term = jnp.dot(weight, v, preferred_element_type=jnp.float32)
-                partial[side, i, j * chunk : (j + 1) * chunk, :] = term.astype(jnp.bfloat16)
+                span = slice(j * chunk, (j + 1) * chunk)
+                partial[side, i, span, :] = (term * seen[side, block, span, :]).astype(jnp.bfloat16)
 
         return carry
 
@@ -237,66 +279,110 @@
 
     def term_of(zd, xd, e):
         total = None
-        tile = xd * 16 + zd * 2 + core
         for side in range(2):
-            other = core if side == 0 else 1 - core
             for b in range(2):
-                block = (hist - core + other) * 2 + b
-                m = bmask[tile, block].astype(jnp.float32)
-                s = msg_s[side, 8 + b * H + e, 0]
-                part = partial[side, s, pl.ds(pl.multiple_of(zd * 128 + xd * 64, 64), TILE), :]
-                part = part.astype(jnp.float32) * m
+                part = partial[side, msg_s[side, 8 + b * H + e, 0], pl.ds(pl.multiple_of(zd * 128 + xd * 64, 64), TILE), :]
+                part = part.astype(jnp.float32)
                 total = part if total is None else total + part
         return total
 
-    def sum_copy(g, s, j):
+    def offset_of(g, s):
+        return 4 - s if g == 0 else 4 + s
+
+    def heads_of(g, s):
+        return range(4) if s else range(2 * g, 2 * g + 2)
+
+    def za_copy(g, s, j):
+        part = pl.ds(heads_of(g, s)[0], len(heads_of(g, s)))
         return remote(
-            rs_send.at[g, s, j], rs_recv.at[g, s, j], sum_send.at[g, s, j], sum_recv.at[g, s, j], up if g == 0 else down
+            za_send.at[g, s, j, part], za_recv.at[g, s, j, part], za_ssem.at[g, s, j], za_rsem.at[g, s, j], (up, down)[g]
         )
 
-    def ring_step(s, arrived):
+    def zb_copy(g, s):
+        part = pl.ds(heads_of(g, s)[0], len(heads_of(g, s)))
+        return remote(zb_send.at[g, s, part], zb_recv.at[g, s, part], zb_ssem.at[g, s], zb_rsem.at[g, s], (up, down)[g])
+
+    def xb_copy(o):
+        return remote(xb_send.at[o], xb_recv.at[o], xb_ssem.at[o], xb_rsem.at[o], across)
+
+    def a_step(s):
         for j in range(2):
             for g in range(2):
-                zd = (z + NZ - 1 - s) % NZ if g == 0 else (z + 1 + s) % NZ
-                terms = [term_of(zd, j, g * 4 + e) for e in range(4)]
-                if arrived:
-                    sum_copy(g, s - 1, j).wait_recv()
-                for e in range(4):
-                    cols = slice(e * DH, (e + 1) * DH)
-                    v = terms[e]
-                    if arrived:
-                        v = v + rs_recv[g, s - 1, j, :, cols].astype(jnp.float32)
-                    rs_send[g, s, j, :, cols] = v.astype(jnp.bfloat16)
-                sum_copy(g, s, j).start()
-
-    ring_step(0, False)
-
-    def ring_body(s, carry):
-        ring_step(s, True)
-        return carry
-
-    lax.fori_loop(1, NZ - 1, ring_body, 0)
-    load_w.wait()
+                zd = (z + offset_of(g, s)) % NZ
+                if s:
+                    za_copy(g, s - 1, j).wait_recv()
+                for e in heads_of(g, s):
+                    v = term_of(zd, j, e)
+                    if s and e in heads_of(g, s - 1):
+                        v = v + za_recv[g, s - 1, j, e].astype(jnp.float32)
+                    za_send[g, s, j, e] = v.astype(jnp.bfloat16)
+                za_copy(g, s, j).start()
+
+    def x_step(o):
+        for e in range(4):
+            xb_send[o, e] = term_of((z + o) % NZ, 1 - xh, 4 + e).astype(jnp.bfloat16)
+        xb_copy(o).start()
+
+    def b_step(s):
+        for g in range(2):
+            o = offset_of(g, s)
+            if s or g == 0:
+                xb_copy(o).wait_recv()
+            if s:
+                zb_copy(g, s - 1).wait_recv()
+            for e in heads_of(g, s):
+                v = term_of((z + o) % NZ, xh, 4 + e) + xb_recv[o, e].astype(jnp.float32)
+                if s and e in heads_of(g, s - 1):
+                    v = v + zb_recv[g, s - 1, e].astype(jnp.float32)
+                zb_send[g, s, e] = v.astype(jnp.bfloat16)
+            zb_copy(g, s).start()
+
+    x_step(4)
+    a_step(0)
+    x_step(3)
+    x_step(5)
+    x_step(2)
+    x_step(6)
+    a_step(1)
+    b_step(0)
+    x_step(1)
+    x_step(7)
+    x_step(0)
+    a_step(2)
+    b_step(1)
+    a_step(3)
+    b_step(2)
+
+    def a_final(xd, e):
+        v = term_of(z, xd, e) + za_recv[0, 3, xd, e].astype(jnp.float32)
+        return v + za_recv[1, 3, xd, e].astype(jnp.float32)
+
     for j in range(2):
         for g in range(2):
-            sum_copy(g, NZ - 2, j).wait_recv()
-
-    def final_terms(xd):
-        out = []
-        for e in range(H):
-            g, cols = e // 4, slice(e % 4 * DH, (e % 4 + 1) * DH)
-            out.append(term_of(z, xd, e) + rs_recv[g, NZ - 2, xd, :, cols].astype(jnp.float32))
-        return out
-
-    for e, v in enumerate(final_terms(1 - xh)):
-        xs_send[:, e * DH : (e + 1) * DH] = v.astype(jnp.bfloat16)
-    x_copy = remote(xs_send, xs_recv, x_sem.at[0], x_sem.at[1], across)
-    x_copy.start()
-    for e, v in enumerate(final_terms(xh)):
+            za_copy(g, 3, j).wait_recv()
+    for e in range(4):
+        xa_send[e] = a_final(1 - xh, e).astype(jnp.bfloat16)
+    xa_copy = remote(xa_send, xa_recv, xa_sem.at[0], xa_sem.at[1], across)
+    xa_copy.start()
+    b_step(3)
+    for e in range(4):
         cols = slice(e * DH, (e + 1) * DH)
+        own_term[:, cols] = own_term[:, cols] + a_final(xh, e)
+    load_w.wait()
+    load_count.wait()
+    xa_copy.wait()
+    for e in range(4):
+        cols = slice(e * DH, (e + 1) * DH)
+        own_term[:, cols] = own_term[:, cols] + xa_recv[e].astype(jnp.float32)
+    xb_copy(0).wait_recv()
+    for g in range(2):
+        zb_copy(g, 3).wait_recv()
+    for e in range(4):
+        cols = slice((4 + e) * DH, (5 + e) * DH)
+        v = term_of(z, xh, 4 + e) + xb_recv[0, e].astype(jnp.float32)
+        v = v + zb_recv[0, 3, e].astype(jnp.float32) + zb_recv[1, 3, e].astype(jnp.float32)
         own_term[:, cols] = own_term[:, cols] + v
-    x_copy.wait()
-    attn = own_term[...] + xs_recv[...].astype(jnp.float32)
+    attn = own_term[...]
     centre = attn - jnp.mean(attn, axis=1, keepdims=True)
     variance = jnp.mean(centre * centre, axis=1, keepdims=True)
     mixed = (centre * lax.rsqrt(variance + 1e-05) * gain[...] * gating[...]).astype(jnp.bfloat16)
@@ -319,29 +405,31 @@
 
     lax.fori_loop(0, CAP, drain_pages, 0)
 
-    def drain_sums(s, carry):
+    for s in range(4):
         for g in range(2):
             for j in range(2):
-                sum_copy(g, s, j).wait_send()
-        return carry
-
-    lax.fori_loop(0, NZ - 1, drain_sums, 0)
+                za_copy(g, s, j).wait_send()
+            zb_copy(g, s).wait_send()
+    for o in range(NZ):
+        xb_copy(o).wait_send()
 
 
 def body(proj, cache, owner, page, length, count, bmask, gain, w_out):
     vmem, smem = pl.BlockSpec(memory_space=pltpu.VMEM), pl.BlockSpec(memory_space=pltpu.SMEM)
     anywhere = pl.BlockSpec(memory_space=pl.ANY)
-    owner_col = owner[0]
-    owner_row = jnp.pad(owner.reshape(1, 16), ((0, 0), (0, 112)), constant_values=-1)
-    page_col = page.reshape(16, 1)
     dma = pltpu.SemaphoreType.DMA
     bf, f32, i32 = jnp.bfloat16, jnp.float32, jnp.int32
     out = pl.pallas_call(
         kernel,
         out_shape=jax.ShapeDtypeStruct((TILE, D), bf),
-        in_specs=[smem, smem, smem, vmem, vmem, vmem, vmem, vmem, anywhere, anywhere],
+        in_specs=[anywhere, anywhere, smem, smem, vmem, anywhere, anywhere, anywhere, anywhere],
         out_specs=vmem,
         scratch_shapes=[
+            pltpu.SMEM((1,), i32),
+            pltpu.SMEM((1,), i32),
+            pltpu.SMEM((32, 64), i32),
+            pltpu.VMEM((2, 2, 1024, DH), f32),
+            pltpu.VMEM((TILE, 4 * D), bf),
             pltpu.VMEM((16, BLK, 2 * DH), bf),
             pltpu.VMEM((D, D), bf),
             pltpu.VMEM((SLOTS, BLK, 2 * DH), bf),
@@ -354,11 +442,15 @@
             pltpu.VMEM((PEERS, 8, 128), i32),
             pltpu.SMEM((2, 24, 128), i32),
             pltpu.SMEM((PEERS, 8, 128), i32),
-            pltpu.VMEM((2, NZ - 1, 2, TILE, D // 2), bf),
-            pltpu.VMEM((2, NZ - 1, 2, TILE, D // 2), bf),
-            pltpu.VMEM((TILE, D), bf),
-            pltpu.VMEM((TILE, D), bf),
-            dma((4,)),
+            pltpu.VMEM((2, 4, 2, 4, TILE, DH), bf),
+            pltpu.VMEM((2, 4, 2, 4, TILE, DH), bf),
+            pltpu.VMEM((2, 4, 4, TILE, DH), bf),
+            pltpu.VMEM((2, 4, 4, TILE, DH), bf),
+            pltpu.VMEM((NZ, 4, TILE, DH), bf),
+            pltpu.VMEM((NZ, 4, TILE, DH), bf),
+            pltpu.VMEM((4, TILE, DH), bf),
+            pltpu.VMEM((4, TILE, DH), bf),
+            dma((8,)),
             dma((PEERS,)),
             dma((PEERS,)),
             dma((SLOTS,)),
@@ -368,15 +460,19 @@
             dma((2,)),
             dma((2, 5)),
             dma((2, 5)),
-            dma((2, NZ - 1, 2)),
-            dma((2, NZ - 1, 2)),
+            dma((2, 4, 2)),
+            dma((2, 4, 2)),
+            dma((2, 4)),
+            dma((2, 4)),
+            dma((NZ,)),
+            dma((NZ,)),
             dma((2,)),
         ],
         compiler_params=pltpu.CompilerParams(
             collective_id=0, has_side_effects=True, vmem_limit_bytes=60 * 1024 * 1024
         ),
         name="score_candidates",
-    )(length, count, bmask[0], proj[0], owner_col, owner_row, page_col, gain.reshape(1, D), cache[0], w_out)
+    )(length, count, owner.reshape(1, 16), page, gain.reshape(1, D), bmask[0], proj[0], cache[0], w_out)
     return out[None]
 
 

time: 133 us -> 117 us (0.88)
  Pallas kernels: 126 us -> 114 us
  local copies, waits for them, and re-layouts: 5.46 us -> 1.57 us
    pallas_call x1, Pallas kernels: 126 us -> 114 us  [body(): pl.pallas_call(kernel, out_shape=jax.ShapeDtypeStruct((TILE, D), bf), in_...]
where the time goes in v2:
time: 117 us
  Pallas kernels  114 us (97%)
  local copies, waits for them, and re-layouts  1.57 us (1%)
  between operations  1.3 us (1%)
    pallas_call x1, Pallas kernels, body(): pl.pallas_call(kernel, out_shape=jax.ShapeDtypeStruct((TILE, D), bf), in_...  114 us

profile of v2, /device:TPU:8, one launch (start us, length us, event | category | flops | bytes accessed | tf_op | source)
XLA Modules:
  0.0 116.7 jit_solution(11394763435321971698)
XLA Ops:
  1.3 113.9 %score_candidates.1 = bf16[64,1024]{1,0:T(8,128)(2,1)} custom-call(s32[1]{0:T(128)S(6)} %copy.11.length_hbm, s32[1]{0:T(128)S(6)} %copy.12.count_hbm, s32[1,16]{1,0:T(1,128)} %bitcast.11, s32[1,16]{1,0:T(1,128)} %page_ref.1, f32[1,1024]{1,0:T(1,128)} %bitcast.10, s32[32,64]{1,0:T(8,128)} %bitcast.9, bf16[64,4096]{1,0:T(8,128)(2,1)} %bitcast.7, ...), custom_call_target="tpu_custom_call" | custom-call | tf_op jit(solution)/shard_map/score_candidates/pallas_call | solution.py:422
  115.2 1.6 %copy.13 = bf16[1,64,1024]{2,1,0:T(8,128)(2,1)} copy(bf16[1,64,1024]{2,1,0:T(8,128)(2,1)} %bitcast.8) | data formatting | bytes 262144

commit v3 on v2

--- a/solution.py
+++ b/solution.py
@@ -16,7 +16,8 @@
 CAP = 3
 PAGES = 16
 SLOTS = PEERS * CAP
-LAG = 2
+LAG = 1
+ORDER = (0, 4, 1, 3, 5, 7, 2, 6)
 SCALE = DH ** (-0.5)
 MESH = pl.DeviceIdType.MESH
 
@@ -131,7 +132,10 @@
     same = (owners == owners_across) & (lane < row)
     rank = jnp.minimum(jnp.sum(same.astype(jnp.int32), axis=1, keepdims=True), CAP - 1)
     place = (((owners >> 2) ^ xl) & 1) * NY + ((owners - y) & 3)
-    slot = jnp.broadcast_to(rank, (16, 128)) * PEERS + place
+    turn = zero
+    for n in range(1, PEERS):
+        turn = jnp.where(place == ORDER[n], n, turn)
+    slot = jnp.broadcast_to(rank, (16, 128)) * PEERS + turn
     match = slot == lane
     load_length.wait()
     valid = jnp.clip(length_ref[0] - (hist * 2 + (row >> 3)) * BLK, 0, BLK)
@@ -170,14 +174,14 @@
     load_cache.wait()
     copy_asked.wait()
 
-    def page_copy(k, d):
-        i = k * PEERS + d
+    def page_copy(i, d):
         return remote(stage.at[i], pages.at[0, i], page_send.at[i], page_recv.at[i], asker_at(d))
 
     def serve(k, carry):
-        for d in (4, 1, 3, 5, 7, 2, 6):
-            stage[k * PEERS + d] = cache_v[asked_s[d, 0, k * PEERS + d]]
-            page_copy(k, d).start()
+        for n in range(1, PEERS):
+            i, d = k * PEERS + n, ORDER[n]
+            stage[i] = cache_v[asked_s[d, 0, i]]
+            page_copy(i, d).start()
         return carry
 
     lax.fori_loop(0, CAP, serve, 0)
@@ -247,7 +251,7 @@
         def _():
             @pl.when((side == 0) & (i % PEERS != 0))
             def _():
-                page_copy(0, i).wait_recv()
+                page_copy(i, 1).wait_recv()
 
             @pl.when(side == 0)
             def _():
@@ -397,10 +401,10 @@
             steps[s][direction].wait_send()
 
     def drain_pages(k, carry):
-        for d in range(PEERS):
-            if d:
-                page_copy(k, d).wait_send()
-            pair_copy(k * PEERS + d).wait_send()
+        for n in range(PEERS):
+            if n:
+                page_copy(k * PEERS + n, ORDER[n]).wait_send()
+            pair_copy(k * PEERS + n).wait_send()
         return carry
 
     lax.fori_loop(0, CAP, drain_pages, 0)

time: 117 us -> 113 us (0.966)
  Pallas kernels: 114 us -> 110 us
    pallas_call x1, Pallas kernels: 114 us -> 110 us  [body(): pl.pallas_call(kernel, out_shape=jax.ShapeDtypeStruct((TILE, D), bf), in_...]
where the time goes in v3:
time: 113 us
  Pallas kernels  110 us (97%)
  local copies, waits for them, and re-layouts  1.57 us (1%)
  between operations  1.3 us (1%)
    pallas_call x1, Pallas kernels, body(): pl.pallas_call(kernel, out_shape=jax.ShapeDtypeStruct((TILE, D), bf), in_...  110 us

profile of v3, /device:TPU:8, one launch (start us, length us, event | category | flops | bytes accessed | tf_op | source)
XLA Modules:
  0.0 112.7 jit_solution(10698185408887961263)
XLA Ops:
  1.3 109.9 %score_candidates.1 = bf16[64,1024]{1,0:T(8,128)(2,1)} custom-call(s32[1]{0:T(128)S(6)} %copy.11.length_hbm, s32[1]{0:T(128)S(6)} %copy.12.count_hbm, s32[1,16]{1,0:T(1,128)} %bitcast.11, s32[1,16]{1,0:T(1,128)} %page_ref.1, f32[1,1024]{1,0:T(1,128)} %bitcast.10, s32[32,64]{1,0:T(8,128)} %bitcast.9, bf16[64,4096]{1,0:T(8,128)(2,1)} %bitcast.7, ...), custom_call_target="tpu_custom_call" | custom-call | tf_op jit(solution)/shard_map/score_candidates/pallas_call | solution.py:426
  111.2 1.6 %copy.13 = bf16[1,64,1024]{2,1,0:T(8,128)(2,1)} copy(bf16[1,64,1024]{2,1,0:T(8,128)(2,1)} %bitcast.8) | data formatting | bytes 262144

commit v4 on v3

--- a/solution.py
+++ b/solution.py
@@ -17,7 +17,7 @@
 PAGES = 16
 SLOTS = PEERS * CAP
 LAG = 1
-ORDER = (0, 4, 1, 3, 5, 7, 2, 6)
+ORDER = (0, 7, 1, 5, 3, 4, 2, 6)
 SCALE = DH ** (-0.5)
 MESH = pl.DeviceIdType.MESH
 

time: 113 us -> 114 us (level)
  no operation moved by 1% of the time
where the time goes in v4:
time: 114 us; the launch traced here: 113 us
  Pallas kernels  110 us (96%)
  local copies, waits for them, and re-layouts  1.57 us (1%)
  between operations  1.3 us (1%)
    pallas_call x1, Pallas kernels, body(): pl.pallas_call(kernel, out_shape=jax.ShapeDtypeStruct((TILE, D), bf), in_...  110 us

profile of v4, /device:TPU:8, one launch (start us, length us, event | category | flops | bytes accessed | tf_op | source)
XLA Modules:
  0.0 112.9 jit_solution(17058333760163131369)
XLA Ops:
  1.3 110.1 %score_candidates.1 = bf16[64,1024]{1,0:T(8,128)(2,1)} custom-call(s32[1]{0:T(128)S(6)} %copy.11.length_hbm, s32[1]{0:T(128)S(6)} %copy.12.count_hbm, s32[1,16]{1,0:T(1,128)} %bitcast.11, s32[1,16]{1,0:T(1,128)} %page_ref.1, f32[1,1024]{1,0:T(1,128)} %bitcast.10, s32[32,64]{1,0:T(8,128)} %bitcast.9, bf16[64,4096]{1,0:T(8,128)(2,1)} %bitcast.7, ...), custom_call_target="tpu_custom_call" | custom-call | tf_op jit(solution)/shard_map/score_candidates/pallas_call | solution.py:426
  111.4 1.6 %copy.13 = bf16[1,64,1024]{2,1,0:T(8,128)(2,1)} copy(bf16[1,64,1024]{2,1,0:T(8,128)(2,1)} %bitcast.8) | data formatting | bytes 262144
